TPU v7x, 128 devices: a whole 4x4x4 slice. The times are simulated.
128 devices in a mesh: grp: 4 (over y), dev: 32 (over z, x, core).
Axes of the slice: x: 4, y: 4, z: 4, core: 2. Of those that a mesh axis runs over, the one named last changes fastest.
Arguments:
- states: bfloat16 [16, 256, 4096], P('grp', 'dev'), may hold values from -6 to 6
- query_in: bfloat16 [16, 256, 4096], P('grp', 'dev'), may hold values from -6 to 6
- key_in: bfloat16 [16, 256, 1024], P('grp', 'dev'), may hold values from -6 to 6
- value_in: bfloat16 [16, 256, 1024], P('grp', 'dev'), may hold values from -6 to 6
- cached_delta: bfloat16 [16, 256, 4096], P('grp', 'dev'), may hold values from -4 to 4
- recompute: int32 [16], P('grp'), may hold values from 0 to 1, as said below
- expert_ids: int32 [4096, 8], P(('grp', 'dev')), may hold values from 0 to 31, as said below
- expert_weights: float32 [4096, 8], P(('grp', 'dev')), may hold values from 0.1 to 1
- norm_gain: float32 [4096], replicated, may hold values from 0.1 to 1.9
- out_proj: bfloat16 [4096, 4096], P('dev'), may hold values from -0.5 to 0.5
- gate_proj: bfloat16 [32, 4096, 3072], P('dev', None, 'grp'), may hold values from -0.09375 to 0.09375
- up_proj: bfloat16 [32, 4096, 3072], P('dev', None, 'grp'), may hold values from -0.09375 to 0.09375
- down_proj: bfloat16 [32, 3072, 4096], P('dev', 'grp'), may hold values from -0.109375 to 0.109375
Outputs:
- layer_out: bfloat16 [16, 256, 4096], P('grp', 'dev')
Inputs may be any that keep to these rules, and one draw needn't show every extreme that they name: `recompute`: 1 marks a recomputed request, 0 one whose cached change is reused; the 4 consecutive requests of one index of grp hold 2 to 3 recomputed ones, and some index holds exactly 3. `expert_ids`: each row names 8 different experts; in each aligned block of 32 rows (the rows of one device) no expert is named by more than 10 rows, and some expert by exactly 10.
All inputs are finite; a program needn't handle non-finite values.
Results may differ from a plain program's by a relative error of at most 0.024.
Values may be sent and summed in bfloat16 or wider, within the bound.
A program may use at most 128 MiB of HBM per device.

v0:
```python
import math

import jax
import jax.numpy as jnp
from jax import lax
from jax.sharding import PartitionSpec as P

HEADS = 32
KV_HEADS = 8
DH = 128


def attend(packed):
    query_part = packed[..., :DH]
    key_part = packed[..., DH : 2 * DH]
    value_part = packed[..., 2 * DH :]
    scores = jnp.einsum(
        "aqhd,akhd->ahqk", query_part, key_part, preferred_element_type=jnp.float32
    ) * (1.0 / math.sqrt(DH))
    highest = jnp.max(scores, axis=-1, keepdims=True)
    raised = jnp.exp(scores - highest)
    attn_weights = (raised / jnp.sum(raised, axis=-1, keepdims=True)).astype(jnp.bfloat16)
    return jnp.einsum(
        "ahqk,akhd->aqhd", attn_weights, value_part, preferred_element_type=jnp.float32
    ).astype(jnp.bfloat16)


def on_device(
    states,
    query_in,
    key_in,
    value_in,
    cached_delta,
    recompute,
    expert_ids,
    expert_weights,
    norm_gain,
    out_proj,
    gate_proj,
    up_proj,
    down_proj,
):
    dev_count = lax.axis_size("dev")
    req_here, seq_here, features = states.shape
    repeat_factor = HEADS // KV_HEADS
    query_sel, key_sel, value_sel = (query_in, key_in, value_in)
    picked_count = query_sel.shape[0]
    queries = query_sel.reshape(picked_count, seq_here, HEADS, DH)
    keys_wide = jnp.repeat(
        key_sel.reshape(picked_count, seq_here, KV_HEADS, DH), repeat_factor, axis=2
    )
    values_wide = jnp.repeat(
        value_sel.reshape(picked_count, seq_here, KV_HEADS, DH), repeat_factor, axis=2
    )
    stacked = jnp.concatenate([queries, keys_wide, values_wide], axis=3)
    attended = attend(lax.all_to_all(stacked, "dev", split_axis=2, concat_axis=1, tiled=True))
    local_heads = attended.shape[2]
    gathered_rows = (
        attended.reshape(picked_count, dev_count, seq_here, local_heads * DH)
        .transpose(1, 0, 2, 3)
        .reshape(dev_count * picked_count * seq_here, local_heads * DH)
    )
    projected = (
        lax.psum_scatter(
            jnp.dot(gathered_rows, out_proj, preferred_element_type=jnp.float32).astype(
                jnp.bfloat16
            ),
            "dev",
            scatter_dimension=0,
            tiled=True,
        )
        .astype(jnp.float32)
        .reshape(picked_count, seq_here, features)
    )
    residual = states.astype(jnp.float32) + projected
    rows_total = req_here * seq_here
    mean_square = jnp.mean(residual * residual, axis=-1, keepdims=True)
    normed = (
        (residual * lax.rsqrt(mean_square + 1e-06) * norm_gain)
        .astype(jnp.bfloat16)
        .reshape(rows_total, features)
    )
    top_count = expert_ids.shape[1]
    capacity = min(rows_total, 5 * rows_total * top_count // (4 * dev_count))
    live_rows = jnp.repeat(recompute, seq_here)
    pair_live = jnp.repeat(live_rows, top_count) == 1
    flat_ids = expert_ids.reshape(-1)
    one_hot = (
        (flat_ids[:, None] == jnp.arange(dev_count, dtype=jnp.int32)[None, :]) & pair_live[:, None]
    ).astype(jnp.int32)
    earlier = jnp.cumsum(one_hot, axis=0) - one_hot
    slot_index = jnp.sum(earlier * one_hot, axis=1)
    target = jnp.where(pair_live, flat_ids * capacity + slot_index, dev_count * capacity)
    source_row = jnp.arange(rows_total * top_count, dtype=jnp.int32) // top_count
    lookup = (
        jnp.full((dev_count * capacity,), rows_total, jnp.int32)
        .at[target]
        .set(source_row, mode="drop")
    )
    padded_rows = jnp.concatenate([normed, jnp.zeros((1, features), jnp.bfloat16)], axis=0)
    outgoing = jnp.take(padded_rows, lookup, axis=0).reshape(dev_count, capacity, features)
    gate_local = gate_proj[0]
    up_local = up_proj[0]
    down_local = down_proj[0]
    arrived = lax.all_to_all(outgoing, "dev", split_axis=0, concat_axis=0, tiled=True)
    every_group = lax.all_gather(arrived, "grp", axis=0, tiled=True).reshape(-1, features)
    gate_val = jnp.dot(every_group, gate_local, preferred_element_type=jnp.float32)
    up_val = jnp.dot(every_group, up_local, preferred_element_type=jnp.float32)
    hidden_val = (jax.nn.silu(gate_val) * up_val).astype(jnp.bfloat16)
    summed = lax.psum_scatter(
        jnp.dot(hidden_val, down_local, preferred_element_type=jnp.float32).astype(jnp.bfloat16),
        "grp",
        scatter_dimension=0,
        tiled=True,
    )
    finished = summed.reshape(dev_count, capacity, features)
    returned = lax.all_to_all(finished, "dev", split_axis=0, concat_axis=0, tiled=True)
    picked = jnp.take(
        returned.reshape(dev_count * capacity, features),
        jnp.minimum(target, dev_count * capacity - 1),
        axis=0,
    ).reshape(rows_total, top_count, features)
    route_weight = jnp.where(pair_live, expert_weights.reshape(-1), 0.0).reshape(
        rows_total, top_count
    )
    mixture = jnp.sum(route_weight[:, :, None] * picked.astype(jnp.float32), axis=1)
    reused = (states.astype(jnp.float32) + cached_delta.astype(jnp.float32)).reshape(
        rows_total, features
    )
    layer_out = jnp.where(
        (live_rows == 1)[:, None], residual.reshape(rows_total, features) + mixture, reused
    )
    return layer_out.astype(jnp.bfloat16).reshape(req_here, seq_here, features)


def solution(mesh):
    return jax.shard_map(
        on_device,
        mesh=mesh,
        in_specs=(
            P("grp", "dev", None),
            P("grp", "dev", None),
            P("grp", "dev", None),
            P("grp", "dev", None),
            P("grp", "dev", None),
            P("grp"),
            P(("grp", "dev"), None),
            P(("grp", "dev"), None),
            P(),
            P("dev", None),
            P("dev", None, "grp"),
            P("dev", None, "grp"),
            P("dev", "grp", None),
        ),
        out_specs=P("grp", "dev", None),
        check_vma=False,
    )
```

profile of v0, /device:TPU:1, one launch (start us, length us, event | category | flops | bytes accessed | tf_op | source)
XLA Modules:
  0.0 551.7 jit_solution(4046249671554310122)
XLA Ops:
  6.5 0.9 copy.41
  7.5 0.9 copy.42
  8.3 1.0 copy.63
  9.9 23.5 %all_to_all.28 = bf16[4,8,32,384]{3,1,0,2:T(8,128)(2,1)S(1)} all-to-all(bf16[4,8,32,384]{3,1,0,2:T(8,128)(2,1)S(1)} %copy.43), channel_id=1, replica_groups=mesh['grp'=4,'dev'=32] {'dev'}, dimensions={2} | all-to-all | bytes 1572864 | tf_op jit(solution)/shard_map/all_to_all | solution.py:56
  33.4 0.5 fusion.31
  33.9 0.7 fusion.14
  34.9 5.6 %convolution_convert_fusion.1 = bf16[1024,4096]{1,0:T(8,128)(2,1)} fusion(bf16[1024,128]{1,0:T(8,128)(2,1)S(1)} %bitcast.109, bf16[128,4096]{1,0:T(8,128)(2,1)S(1)} %copy-done), kind=kOutput, calls=%fused_computation.5 | convolution fusion | flops 1077936128 | bytes 9699328 | tf_op jit(solution)/shard_map/dot_general | solution.py:65
  40.5 0.6 copy-done.5
  42.3 0.6 reduce-window.6
  43.3 1.4 scatter_custom_fusion
  44.9 84.5 %reduce-scatter.3.cloned.1.call-done = bf16[32,4096]{1,0:T(8,128)(2,1)} async-done(((bf16[1024,4096]{1,0:T(8,128)(2,1)}), bf16[32,4096]{1,0:T(8,128)(2,1)}) %reduce-scatter.3.cloned.1.call-update) | async-done | bytes 262160 | tf_op jit(solution)/shard_map/reduce_scatter | solution.py:64
  129.5 1.1 multiply_reduce_fusion.1
  130.6 1.1 fusion.17
  131.7 3.9 gather_fusion
  135.6 4.6 gather.13
  140.2 2.6 broadcast_select_fusion
  142.8 58.0 %all_to_all.29 = bf16[32,10,4096]{2,1,0:T(8,128)(2,1)S(1)} all-to-all(bf16[32,10,4096]{2,1,0:T(8,128)(2,1)S(1)} %broadcast_select_fusion), channel_id=1, replica_groups=mesh['grp'=4,'dev'=32] {'dev'}, dimensions={0} | all-to-all | bytes 5242880 | tf_op jit(solution)/shard_map/all_to_all | solution.py:105
  200.8 2.9 copy.54
  204.0 98.2 %all-gather.2.cloned.1.call-done = bf16[128,10,4096]{2,0,1:T(8,128)(2,1)} async-done(((bf16[32,10,4096]{2,0,1:T(8,128)(2,1)}), bf16[128,10,4096]{2,0,1:T(8,128)(2,1)}) %all-gather.2.cloned.1.call-update) | async-done | bytes 10485776 | tf_op jit(solution)/shard_map/all_gather | solution.py:106
  302.2 15.2 %copy.55 = bf16[128,10,4096]{2,1,0:T(8,128)(2,1)} copy(bf16[128,10,4096]{2,0,1:T(8,128)(2,1)} %all-gather.2.cloned.1.call-done) | data formatting | bytes 20971520 | tf_op jit(solution)/shard_map/all_gather | solution.py:106
  317.4 16.7 %reshape.261 = bf16[1280,4096]{1,0:T(8,128)(2,1)} reshape(bf16[128,10,4096]{2,1,0:T(8,128)(2,1)} %copy.55) | data formatting | bytes 20971520 | tf_op jit(solution)/shard_map/reshape | solution.py:106
  334.1 12.3 %fusion.4 = f32[1280,768]{1,0:T(8,128)S(1)} fusion(bf16[1280,4096]{1,0:T(8,128)(2,1)} %reshape.261, bf16[1,4096,768]{2,1,0:T(8,128)(2,1)} %param.23), kind=kOutput, calls=%fused_computation.9 | convolution fusion | flops 8053063680 | bytes 20709376 | tf_op jit(solution)/shard_map/dot_general | solution.py:107
  346.4 9.0 %fusion.9 = bf16[1280,768]{1,0:T(8,128)(2,1)S(1)} fusion(bf16[1280,4096]{1,0:T(8,128)(2,1)S(1)} %copy-done.2, bf16[1,4096,768]{2,1,0:T(8,128)(2,1)S(1)} %bitcast.120, f32[1280,768]{1,0:T(8,128)S(1)} %fusion.4), kind=kOutput, calls=%fused_computation.14 | convolution fusion | flops 8058961920 | bytes 22675456 | tf_op jit(solution)/shard_map/dot_general | solution.py:108
  355.4 13.8 %convolution_convert_fusion = bf16[1280,4096]{1,0:T(8,128)(2,1)} fusion(bf16[1280,768]{1,0:T(8,128)(2,1)S(1)} %fusion.9, bf16[1,768,4096]{2,1,0:T(8,128)(2,1)} %param.25), kind=kOutput, calls=%fused_computation.4 | convolution fusion | flops 8058306560 | bytes 18743296 | tf_op jit(solution)/shard_map/dot_general | solution.py:111
  369.2 98.7 %reduce-scatter.5.cloned.1.call-done = bf16[320,4096]{1,0:T(8,128)(2,1)} async-done(((bf16[1280,4096]{1,0:T(8,128)(2,1)}), bf16[320,4096]{1,0:T(8,128)(2,1)}) %reduce-scatter.5.cloned.1.call-update) | async-done | bytes 2621456 | tf_op jit(solution)/shard_map/reduce_scatter | solution.py:110
  467.9 4.6 reshape.262
  472.5 7.8 %all-to-all-start.2 = ((bf16[32,10,4096]{2,1,0:T(8,128)(2,1)}), bf16[32,10,4096]{2,1,0:T(8,128)(2,1)}, u32[]{:S(2)}, u32[]{:S(2)}) async-start(bf16[32,10,4096]{2,1,0:T(8,128)(2,1)} %reshape.262), calls=%async_computation.4 | async-start | bytes 8388608 | tf_op jit(solution)/shard_map/all_to_all | solution.py:117
  480.7 49.9 %all-to-all-done.2 = bf16[32,10,4096]{2,1,0:T(8,128)(2,1)} async-done(((bf16[32,10,4096]{2,1,0:T(8,128)(2,1)}), bf16[32,10,4096]{2,1,0:T(8,128)(2,1)}, u32[]{:S(2)}, u32[]{:S(2)}) %all-to-all-start.2) | async-done | bytes 2621472 | tf_op jit(solution)/shard_map/all_to_all | solution.py:117
  530.6 4.7 reshape.263
  535.3 6.0 %gather_fusion.1 = bf16[256,4096]{1,0:T(8,128)(2,1)S(1)} fusion(bf16[320,4096]{1,0:T(8,128)(2,1)} %reshape.263, s32[1024]{0:T(1024)S(1)} %pad_clamp_fusion), kind=kCustom, calls=%fused_computation.1 | custom fusion | bytes 4195328 | tf_op jit(solution)/shard_map/jit(_take)/gather | solution.py:118
  541.3 1.9 multiply_reduce_fusion
  543.2 1.9 fusion.16
  (67 shorter events, 3.2 us)
Async XLA Ops:
  6.5 28.3 %copy-start = (bf16[128,4096]{1,0:T(8,128)(2,1)S(1)}, bf16[128,4096]{1,0:T(8,128)(2,1)}, u32[]{:S(2)}) copy-start(bf16[128,4096]{1,0:T(8,128)(2,1)} %param.22) | copy-start | bytes 3145732
  6.5 122.9 %reduce-scatter.3.cloned.1.call-start = ((), (), s32[]{:S(2)}) async-start(), calls=%async_computation.5 | async-start | bytes 8650752 | tf_op jit(solution)/shard_map/reduce_scatter | solution.py:64
  40.4 0.7 copy-start.5
  40.5 0.9 copy-start.7
  40.5 89.0 %copy-start.3 = (bf16[4,8,4096]{2,1,0:T(8,128)(2,1)S(1)}, bf16[4,8,4096]{2,1,0:T(8,128)(2,1)}, u32[]{:S(2)}) copy-start(bf16[4,8,4096]{2,1,0:T(8,128)(2,1)} %param.13) | copy-start | bytes 786436
  40.5 90.1 %copy-start.4 = (f32[4096]{0:T(1024)S(1)}, f32[4096]{0:T(1024)}, u32[]{:S(2)}) copy-start(f32[4096]{0:T(1024)} %param.21) | copy-start | bytes 49156
  40.5 261.7 %all-gather.2.cloned.1.call-start = ((), (), s32[]{:S(2)}) async-start(), calls=%async_computation.6 | async-start | bytes 13107200 | tf_op jit(solution)/shard_map/all_gather | solution.py:106
  203.7 264.2 %reduce-scatter.5.cloned.1.call-start = ((), (), s32[]{:S(2)}) async-start(), calls=%async_computation.7 | async-start | bytes 13107200 | tf_op jit(solution)/shard_map/reduce_scatter | solution.py:110
  317.4 29.0 %slice-start = ((s8[6291456]{0:T(1024)(128)(4,1)}), s8[2097152]{0:T(1024)(128)(4,1)S(1)}, s32[]{:S(2)}) async-start(s8[6291456]{0:T(1024)(128)(4,1)} %bitcast.119), calls=%async_computation.8 | async-start | bytes 4194304
  334.1 12.3 %copy-start.2 = (bf16[1280,4096]{1,0:T(8,128)(2,1)S(1)}, bf16[1280,4096]{1,0:T(8,128)(2,1)}, u32[]{:S(2)}) copy-start(bf16[1280,4096]{1,0:T(8,128)(2,1)} %reshape.261) | copy-start | bytes 31457284
  334.1 12.3 %slice-start.1 = ((s8[6291456]{0:T(1024)(128)(4,1)}), s8[4194304]{0:T(1024)(128)(4,1)S(1)}, s32[]{:S(2)}) async-start(s8[6291456]{0:T(1024)(128)(4,1)} %bitcast.119), calls=%async_computation.9 | async-start | bytes 8388608
  472.5 7.9 %copy-start.6 = (f32[32,8]{0,1:T(8,128)S(1)}, f32[32,8]{0,1:T(8,128)}, u32[]{:S(2)}) copy-start(f32[32,8]{0,1:T(8,128)} %param.20) | copy-start | bytes 3076
  472.5 58.1 %all-to-all-start.2 = ((bf16[32,10,4096]{2,1,0:T(8,128)(2,1)}), bf16[32,10,4096]{2,1,0:T(8,128)(2,1)}, u32[]{:S(2)}, u32[]{:S(2)}) async-start(bf16[32,10,4096]{2,1,0:T(8,128)(2,1)} %reshape.262), calls=%async_computation.4 | async-start | bytes 8388608 | tf_op jit(solution)/shard_map/all_to_all | solution.py:117
  535.3 9.9 %copy-start.1 = (bf16[128,4096]{1,0:T(8,128)(2,1)S(1)}, bf16[128,4096]{1,0:T(8,128)(2,1)}, u32[]{:S(2)}) copy-start(bf16[128,4096]{1,0:T(8,128)(2,1)} %param.22) | copy-start | bytes 3145732
Sparse Core Ops, SparseCore 0:
  40.6 88.7 reduce-scatter.2
  203.9 98.2 all-gather.1
  369.3 98.5 reduce-scatter.4
where the time goes:
time: 555 us; the launch traced here: 552 us
  waiting for transfers between devices  331 us (60%)
  blocking collectives  81.4 us (15%)
  local copies, waits for them, and re-layouts  65.9 us (12%)
  matrix products  41.8 us (8%)
  between operations  13.4 us (2%)
  other arithmetic  9.67 us (2%)
  starting transfers between devices  8.05 us (1%)
    reduce_scatter x1, waiting for transfers between devices, on_device(): lax.psum_scatter(jnp.dot(hidden_val, down_local, preferred_element_type=j...  98.7 us
    all_gather x1, waiting for transfers between devices, on_device(): lax.all_gather(arrived, 'grp', axis=0, tiled=True).reshape(-1, features)  98.2 us
    reduce_scatter x1, waiting for transfers between devices, on_device(): lax.psum_scatter(jnp.dot(gathered_rows, out_proj, preferred_element_type=...  84.5 us
    all_to_all x1, blocking collectives, on_device(): lax.all_to_all(outgoing, 'dev', split_axis=0, concat_axis=0, tiled=True)  58 us
    all_to_all x1, waiting for transfers between devices, on_device(): lax.all_to_all(finished, 'dev', split_axis=0, concat_axis=0, tiled=True)  49.9 us
    all_to_all x1, blocking collectives, on_device(): lax.all_to_all(stacked, 'dev', split_axis=2, concat_axis=1, tiled=True)  23.5 us
    reshape x1, local copies, waits for them, and re-layouts, on_device(): lax.all_gather(arrived, 'grp', axis=0, tiled=True).reshape(-1, features)  16.7 us
    all_gather x1, local copies, waits for them, and re-layouts, on_device(): lax.all_gather(arrived, 'grp', axis=0, tiled=True).reshape(-1, features)  15.2 us
  transfers between devices with their start and end apart: 4, of which 4 were waited for; matrix products, arithmetic and copies ran while one was open for 1% of the time, Pallas kernels for 0%

commit v1 on v0

v1 whole, which is shorter than its diff:
```python
import math

import jax
import jax.numpy as jnp
from jax import lax
from jax.experimental import pallas as pl
from jax.experimental.pallas import tpu as pltpu
from jax.sharding import PartitionSpec as P

HEADS = 32
KV_HEADS = 8
DH = 128
SLOTS = 3
BF = jnp.bfloat16
F32 = jnp.float32
MESH = pl.DeviceIdType.MESH
ORDER = (("x", "z", "y"), ("z", "y", "x"), ("y", "x", "z"))


def mod4(v):
    return lax.rem(v + 4, 4)


class Place:
    def __init__(self):
        self.y = lax.axis_index("grp")
        dev = lax.axis_index("dev")
        self.core = lax.rem(dev, 2)
        self.x = lax.rem(lax.div(dev, 2), 4)
        self.z = lax.div(dev, 8)

    def at(self, axis):
        return {"x": self.x, "y": self.y, "z": self.z}[axis]

    def to(self, axis, step):
        y, x, z = self.y, self.x, self.z
        if axis == "y":
            y = mod4(y + step)
        elif axis == "x":
            x = mod4(x + step)
        else:
            z = mod4(z + step)
        return (y, (z * 4 + x) * 2 + self.core)

    def sibling(self):
        return (self.y, (self.z * 4 + self.x) * 2 + 1 - self.core)

    def greet(self, axes):
        barrier = pltpu.get_barrier_semaphore()
        others = [self.to(axis, step) for axis in axes for step in (1, -1)]
        others.append(self.sibling())
        for other in others:
            pl.semaphore_signal(barrier, inc=1, device_id=other, device_id_type=MESH)
        pl.semaphore_wait(barrier, len(others))


class Copies:
    def __init__(self, send_sem, recv_sem):
        self.send_sem, self.recv_sem = send_sem, recv_sem
        self.made = []

    def start(self, src, dst, device):
        k = len(self.made)
        copy = pltpu.make_async_remote_copy(
            src_ref=src,
            dst_ref=dst,
            send_sem=self.send_sem.at[k],
            recv_sem=self.recv_sem.at[k],
            device_id=device,
            device_id_type=MESH,
        )
        copy.start()
        self.made.append(copy)
        return copy

    def finish(self):
        for copy in self.made:
            copy.wait_send()


def gather_kernel(
    norm_ref, gw_ref, gate_hbm, up_hbm, down_hbm,
    hid_out, dsib_out,
    tok, xbuf, wg, wu, hid, send_sem, recv_sem, load_sem, hsend_sem, hrecv_sem, hloc_sem,
):
    here = Place()
    c = here.core
    sib = here.sibling()
    load_g = pltpu.make_async_copy(gate_hbm, wg, load_sem.at[0])
    load_u = pltpu.make_async_copy(up_hbm, wu, load_sem.at[1])
    load_g.start()
    load_u.start()
    here.greet(("x", "y", "z"))
    copies = Copies(send_sem, recv_sem)
    m1 = [here.at(ORDER[p][0]) for p in range(SLOTS)]
    m2 = [here.at(ORDER[p][1]) for p in range(SLOTS)]
    m3 = [here.at(ORDER[p][2]) for p in range(SLOTS)]
    parts = range(SLOTS)

    def to(p, axis_at, step):
        return here.to(ORDER[p][axis_at - 1], step)

    swap = copies.start(norm_ref.at[1 - c], xbuf, sib)
    other_half = pl.ds(pl.multiple_of((1 - c) * 2048, 2048), 2048)
    down_copy = copies.start(down_hbm.at[:, other_half], dsib_out, sib)
    swap.wait_recv()
    pair = pl.ds(2 * c, 2)
    for p in parts:
        mine, others = norm_ref[c, p], xbuf[p]
        low = jnp.where(c == 0, mine, others)
        high = jnp.where(c == 0, others, mine)
        rows = jnp.concatenate([low, high], axis=0).astype(BF)
        tok[2 * c, p, m3[p], m2[p], m1[p]] = rows[:, :1024]
        tok[2 * c + 1, p, m3[p], m2[p], m1[p]] = rows[:, 1024:]

    def send(region, device):
        return copies.start(region, region, device)

    first = []
    for p in parts:
        block = tok.at[pair, p, m3[p], m2[p], m1[p]]
        first.append((send(block, to(p, 1, 1)), send(block, to(p, 1, -1))))
    second = []
    for p in parts:
        for copy in first[p]:
            copy.wait_recv()
        second.append((
            send(tok.at[2 * c, p, m3[p], m2[p], mod4(m1[p] - 1)], to(p, 1, 1)),
            send(tok.at[2 * c + 1, p, m3[p], m2[p], mod4(m1[p] + 1)], to(p, 1, -1)),
        ))

    def line(p, c3, c2):
        return tok.at[pair, p, c3, c2]

    own_line = [{} for p in parts]
    ring2 = []
    subs = [[None] * 4 for p in parts]
    offsets = (0, 1, -1, 2)
    for p in parts:
        for copy in second[p]:
            copy.wait_recv()
        region = line(p, m3[p], m2[p])
        ring2.append((send(region, to(p, 2, 1)), send(region, to(p, 2, -1))))
        own_line[p][0] = send(region, sib)
    for p in parts:
        region = line(p, m3[p], m2[p])
        subs[p][0] = (send(region, to(p, 3, 1)), send(region, to(p, 3, -1)))
    ring2b = []
    for p in parts:
        for copy in ring2[p]:
            copy.wait_recv()
        ring2b.append((
            send(tok.at[2 * c, p, m3[p], mod4(m2[p] - 1)], to(p, 2, 1)),
            send(tok.at[2 * c + 1, p, m3[p], mod4(m2[p] + 1)], to(p, 2, -1)),
        ))
        for j in (1, 2):
            own_line[p][j] = send(line(p, m3[p], mod4(m2[p] + offsets[j])), sib)
    for j in (1, 2):
        for p in parts:
            region = line(p, m3[p], mod4(m2[p] + offsets[j]))
            subs[p][j] = (send(region, to(p, 3, 1)), send(region, to(p, 3, -1)))

    load_g.wait()
    load_u.wait()

    def hid_piece(p, c3, c2):
        return hid.at[p, c3, c2]

    def ffn(pieces):
        def tile(n, carry):
            cols = pl.ds(pl.multiple_of(n * 256, 256), 256)
            gate = jnp.zeros((64 * len(pieces), 256), F32)
            up = jnp.zeros((64 * len(pieces), 256), F32)
            for q in range(4):
                rows = jnp.concatenate([tok[q, p, c3, c2].reshape(64, 1024) for p, c3, c2 in pieces], axis=0)
                depth = pl.ds(q * 1024, 1024)
                gate += jnp.dot(rows, wg[depth, cols], preferred_element_type=F32)
                up += jnp.dot(rows, wu[depth, cols], preferred_element_type=F32)
            act = gate / (1.0 + jnp.exp(-gate)) * up
            for i, (p, c3, c2) in enumerate(pieces):
                weight = gw_ref[p, c3, c2][:, :1]
                hid[p, c3, c2, :, cols] = (act[64 * i : 64 * i + 64] * weight).astype(BF)
            return carry

        lax.fori_loop(0, 3, tile, 0)
        for p, c3, c2 in pieces:
            pltpu.make_async_copy(hid.at[p, c3, c2], hid_out.at[c, p, c3, c2], hloc_sem).start()
            pltpu.make_async_remote_copy(
                src_ref=hid.at[p, c3, c2],
                dst_ref=hid_out.at[c, p, c3, c2],
                send_sem=hsend_sem,
                recv_sem=hrecv_sem,
                device_id=sib,
                device_id_type=MESH,
            ).start()

    def own_unit(lines):
        for p in parts:
            for j in lines:
                own_line[p][j].wait_recv()
        ffn([(p, m3[p], mod4(m2[p] + offsets[j])) for p in parts for j in lines])

    passed = [[None] * 4 for p in parts]
    onward = [[None] * 4 for p in parts]
    opposite = [[None] * 4 for p in parts]

    def forward(j):
        for p in parts:
            line_at = mod4(m2[p] + offsets[j])
            left, right = mod4(m3[p] - 1), mod4(m3[p] + 1)
            for copy in subs[p][j]:
                copy.wait_recv()
            onward[p][j] = (
                send(tok.at[2 * c, p, left, line_at], to(p, 3, 1)),
                send(tok.at[2 * c + 1, p, right, line_at], to(p, 3, -1)),
            )
            passed[p][j] = (send(line(p, left, line_at), sib), send(line(p, right, line_at), sib))

    def near_unit(j):
        for p in parts:
            for copy in passed[p][j]:
                copy.wait_recv()
        ffn([(p, mod4(m3[p] + side), mod4(m2[p] + offsets[j])) for p in parts for side in (-1, 1)])

    def settle(j):
        for p in parts:
            for copy in onward[p][j]:
                copy.wait_recv()
            opposite[p][j] = send(line(p, mod4(m3[p] + 2), mod4(m2[p] + offsets[j])), sib)

    def far_unit(lines):
        for p in parts:
            for j in lines:
                opposite[p][j].wait_recv()
        ffn([(p, mod4(m3[p] + 2), mod4(m2[p] + offsets[j])) for p in parts for j in lines])

    own_unit((0, 1))
    for p in parts:
        for copy in ring2b[p]:
            copy.wait_recv()
        region = line(p, m3[p], mod4(m2[p] + 2))
        subs[p][3] = (send(region, to(p, 3, 1)), send(region, to(p, 3, -1)))
        own_line[p][3] = send(region, sib)
    forward(0)
    own_unit((2, 3))
    forward(1)
    near_unit(0)
    forward(2)
    settle(0)
    near_unit(1)
    forward(3)
    settle(1)
    near_unit(2)
    far_unit((0, 1))
    settle(2)
    near_unit(3)
    settle(3)
    far_unit((2, 3))

    copies.finish()
    down_copy.wait_recv()
    whole = pltpu.make_async_remote_copy(
        src_ref=hid,
        dst_ref=hid_out.at[1 - c],
        send_sem=hsend_sem,
        recv_sem=hrecv_sem,
        device_id=sib,
        device_id_type=MESH,
    )
    whole.wait_send()
    whole.wait_recv()
    pltpu.make_async_copy(hid, hid_out.at[c], hloc_sem).wait()


def expert_hidden(norm_halves, gate_weight, gate_w, up_w, down_w):
    any_space = pl.BlockSpec(memory_space=pl.ANY)
    vmem = pl.BlockSpec(memory_space=pltpu.VMEM)
    count = 2 + SLOTS * (4 + 4 + 16 + 16)
    return pl.pallas_call(
        gather_kernel,
        out_shape=(
            jax.ShapeDtypeStruct((2, SLOTS, 4, 4, 64, 768), BF),
            jax.ShapeDtypeStruct((768, 2048), BF),
        ),
        in_specs=[vmem, vmem, any_space, any_space, any_space],
        out_specs=(any_space, any_space),
        scratch_shapes=[
            pltpu.VMEM((4, SLOTS, 4, 4, 4, 16, 1024), BF),
            pltpu.VMEM((SLOTS, 8, 2048), F32),
            pltpu.VMEM((4096, 768), BF),
            pltpu.VMEM((4096, 768), BF),
            pltpu.VMEM((SLOTS, 4, 4, 64, 768), BF),
            pltpu.SemaphoreType.DMA((count,)),
            pltpu.SemaphoreType.DMA((count,)),
            pltpu.SemaphoreType.DMA((2,)),
            pltpu.SemaphoreType.DMA,
            pltpu.SemaphoreType.DMA,
            pltpu.SemaphoreType.DMA,
        ],
        compiler_params=pltpu.CompilerParams(
            collective_id=1, has_side_effects=True, vmem_limit_bytes=60 * 1024 * 1024
        ),
        name="gather_hidden",
    )(norm_halves, gate_weight, gate_w, up_w, down_w)


def scatter_kernel(
    hid_hbm, down_hbm, dsib_hbm,
    out_ref,
    hv, dw, part_sum, far3, near3, far2, near2, far1, near1, fin,
    send_sem, recv_sem, load_sem,
):
    here = Place()
    c = here.core
    sib = here.sibling()
    parts = range(SLOTS)
    m1 = [here.at(ORDER[p][0]) for p in parts]
    m2 = [here.at(ORDER[p][1]) for p in parts]
    m3 = [here.at(ORDER[p][2]) for p in parts]
    my_half = pl.ds(pl.multiple_of(c * 2048, 2048), 2048)
    loads = {}

    def load(src, dst):
        copy = pltpu.make_async_copy(src, dst, load_sem.at[len(loads)])
        copy.start()
        loads[len(loads)] = copy
        return copy

    loaded_w = [load(down_hbm.at[:, my_half], dw.at[c]), load(dsib_hbm, dw.at[1 - c])]
    planes = (2, 1, -1, 0)
    loaded_h = {}
    for off in planes:
        for p in parts:
            at = mod4(m3[p] + off)
            loaded_h[off, p] = load(hid_hbm.at[:, p, at], hv.at[:, p, at])
    here.greet(("x", "y", "z"))
    copies = Copies(send_sem, recv_sem)

    def to(p, axis_at, step):
        return here.to(ORDER[p][axis_at - 1], step)

    for copy in loaded_w:
        copy.wait()

    def down(p, off):
        at = mod4(m3[p] + off)
        loaded_h[off, p].wait()

        def tile(n, carry):
            cols = pl.ds(pl.multiple_of(n * 512, 512), 512)
            total = jnp.dot(hv[0, p, at].reshape(256, 768), dw[0, :, cols], preferred_element_type=F32)
            total += jnp.dot(hv[1, p, at].reshape(256, 768), dw[1, :, cols], preferred_element_type=F32)
            into = pl.ds(pl.multiple_of(lax.rem(n, 2) * 512, 512), 512)
            part_sum[lax.div(n, 2), p, at, :, :, into] = total.astype(BF).reshape(4, 64, 512)
            return carry

        lax.fori_loop(0, 4, tile, 0)

    def add(ref, *others):
        total = ref[...].astype(F32)
        for other in others:
            total += other[...].astype(F32)
        ref[...] = total.astype(BF)

    lines = (2, 1, -1, 0)

    def at_line(p, k):
        return mod4(m2[p] + lines[k])

    far_copy = {}
    for p in parts:
        down(p, 2)
        at = mod4(m3[p] + 2)
        for k in range(4):
            l = at_line(p, k)
            far_copy[p, k] = (
                copies.start(part_sum.at[0, p, at, l], far3.at[0, p, k], to(p, 3, 1)),
                copies.start(part_sum.at[1, p, at, l], far3.at[1, p, k], to(p, 3, -1)),
            )
    for p in parts:
        down(p, 1)
        down(p, -1)
    near_copy = {}

    def pass_near(k):
        for p in parts:
            l = at_line(p, k)
            right, left = mod4(m3[p] + 1), mod4(m3[p] - 1)
            near_copy[p, k] = [
                copies.start(part_sum.at[1, p, right, l], near3.at[0, 1, p, k], to(p, 3, 1)),
                copies.start(part_sum.at[0, p, left, l], near3.at[1, 0, p, k], to(p, 3, -1)),
            ]
            for copy in far_copy[p, k]:
                copy.wait_recv()
            add(part_sum.at[0, p, right, l], far3.at[0, p, k])
            add(part_sum.at[1, p, left, l], far3.at[1, p, k])
            near_copy[p, k] += [
                copies.start(part_sum.at[0, p, right, l], near3.at[0, 0, p, k], to(p, 3, 1)),
                copies.start(part_sum.at[1, p, left, l], near3.at[1, 1, p, k], to(p, 3, -1)),
            ]

    pass_near(0)
    for p in parts:
        down(p, 0)
    pass_near(1)
    pass_near(2)
    pass_near(3)

    def take_near(p, k):
        for copy in near_copy[p, k]:
            copy.wait_recv()
        for q in range(2):
            add(part_sum.at[q, p, m3[p], at_line(p, k)], near3.at[0, q, p, k], near3.at[1, q, p, k])

    far2_copy, near2_copy = {}, {}
    for p in parts:
        take_near(p, 0)
        l = at_line(p, 0)
        far2_copy[p] = (
            copies.start(part_sum.at[0, p, m3[p], l], far2.at[0, p], to(p, 2, 1)),
            copies.start(part_sum.at[1, p, m3[p], l], far2.at[1, p], to(p, 2, -1)),
        )
    for k, side in ((1, 0), (2, 1)):
        for p in parts:
            take_near(p, k)
            l = at_line(p, k)
            far2_copy[p][side].wait_recv()
            add(part_sum.at[side, p, m3[p], l], far2.at[side, p])
            near2_copy[p, side] = copies.start(
                part_sum.at[:, p, m3[p], l], near2.at[side, :, p], to(p, 2, 1 if side == 0 else -1)
            )
    far1_copy, near1_copy = {}, {}

    def block(p, step):
        return pl.ds(pl.multiple_of(mod4(m1[p] + step) * 16, 16), 16)

    for p in parts:
        take_near(p, 3)
        for side in range(2):
            near2_copy[p, side].wait_recv()
        for q in range(2):
            add(part_sum.at[q, p, m3[p], m2[p]], near2.at[0, q, p], near2.at[1, q, p])
        far1_copy[p] = (
            copies.start(part_sum.at[0, p, m3[p], m2[p], block(p, 2)], far1.at[0, p], to(p, 1, 1)),
            copies.start(part_sum.at[1, p, m3[p], m2[p], block(p, 2)], far1.at[1, p], to(p, 1, -1)),
        )
    for p in parts:
        for side, step in ((0, 1), (1, -1)):
            far1_copy[p][side].wait_recv()
            add(part_sum.at[side, p, m3[p], m2[p], block(p, step)], far1.at[side, p])
            near1_copy[p, side] = copies.start(
                part_sum.at[:, p, m3[p], m2[p], block(p, step)], near1.at[side, :, p], to(p, 1, step)
            )
    for p in parts:
        for side in range(2):
            near1_copy[p, side].wait_recv()
        for q in range(2):
            total = part_sum[q, p, m3[p], m2[p], block(p, 0)].astype(F32)
            total += near1[0, q, p].astype(F32) + near1[1, q, p].astype(F32)
            fin[0, p, :, q * 1024 : q * 1024 + 1024] = total[:8]
            fin[1, p, :, q * 1024 : q * 1024 + 1024] = total[8:]
    last = copies.start(fin.at[1 - c], out_ref.at[c], sib)
    out_ref[c] = fin[c]
    last.wait_recv()
    copies.finish()


def expert_sum(hidden, down_w, down_sib):
    any_space = pl.BlockSpec(memory_space=pl.ANY)
    vmem = pl.BlockSpec(memory_space=pltpu.VMEM)
    count = SLOTS * (8 + 16 + 4 + 4) + 1
    return pl.pallas_call(
        scatter_kernel,
        out_shape=jax.ShapeDtypeStruct((2, SLOTS, 8, 2048), F32),
        in_specs=[any_space, any_space, any_space],
        out_specs=vmem,
        scratch_shapes=[
            pltpu.VMEM((2, SLOTS, 4, 4, 64, 768), BF),
            pltpu.VMEM((2, 768, 2048), BF),
            pltpu.VMEM((2, SLOTS, 4, 4, 64, 1024), BF),
            pltpu.VMEM((2, SLOTS, 4, 64, 1024), BF),
            pltpu.VMEM((2, 2, SLOTS, 4, 64, 1024), BF),
            pltpu.VMEM((2, SLOTS, 64, 1024), BF),
            pltpu.VMEM((2, 2, SLOTS, 64, 1024), BF),
            pltpu.VMEM((2, SLOTS, 16, 1024), BF),
            pltpu.VMEM((2, 2, SLOTS, 16, 1024), BF),
            pltpu.VMEM((2, SLOTS, 8, 2048), F32),
            pltpu.SemaphoreType.DMA((count,)),
            pltpu.SemaphoreType.DMA((count,)),
            pltpu.SemaphoreType.DMA((14,)),
        ],
        compiler_params=pltpu.CompilerParams(
            collective_id=2, has_side_effects=True, vmem_limit_bytes=60 * 1024 * 1024
        ),
        name="down_scatter",
    )(hidden, down_w, down_sib)


def attend(packed):
    query_part = packed[..., :DH]
    key_part = packed[..., DH : 2 * DH]
    value_part = packed[..., 2 * DH :]
    scores = jnp.einsum(
        "aqhd,akhd->ahqk", query_part, key_part, preferred_element_type=jnp.float32
    ) * (1.0 / math.sqrt(DH))
    highest = jnp.max(scores, axis=-1, keepdims=True)
    raised = jnp.exp(scores - highest)
    attn_weights = (raised / jnp.sum(raised, axis=-1, keepdims=True)).astype(jnp.bfloat16)
    return jnp.einsum(
        "ahqk,akhd->aqhd", attn_weights, value_part, preferred_element_type=jnp.float32
    ).astype(jnp.bfloat16)


def on_device(
    states, query_in, key_in, value_in, cached_delta, recompute, expert_ids, expert_weights,
    norm_gain, out_proj, gate_proj, up_proj, down_proj,
):
    dev_count = lax.axis_size("dev")
    req_here, seq_here, features = states.shape
    repeat_factor = HEADS // KV_HEADS
    rank = jnp.cumsum(recompute) - 1
    live_count = jnp.sum(recompute)
    idle_rank = live_count + jnp.cumsum(1 - recompute) - 1
    place = jnp.where(recompute == 1, rank, idle_rank)
    pick = (place[None, :] == jnp.arange(SLOTS, dtype=jnp.int32)[:, None]).astype(jnp.int32)
    chosen = jnp.sum(pick * jnp.arange(req_here, dtype=jnp.int32)[None, :], axis=1)
    live_slot = jnp.arange(SLOTS, dtype=jnp.int32) < live_count

    def select(whole):
        return jnp.concatenate(
            [lax.dynamic_slice_in_dim(whole, chosen[s], 1, 0) for s in range(SLOTS)], axis=0
        )

    ids = select(expert_ids.reshape(req_here, seq_here, -1))
    weights = select(expert_weights.reshape(req_here, seq_here, -1))
    experts = jnp.arange(dev_count, dtype=jnp.int32)
    dense = jnp.sum(
        jnp.where(ids[..., None] == experts, weights[..., None], 0.0), axis=2
    )
    dense = jnp.where(live_slot[:, None, None], dense, 0.0).reshape(SLOTS * seq_here, dev_count)
    all_dense = lax.all_gather(dense, ("grp", "dev"), axis=0, tiled=False)
    mine = lax.dynamic_index_in_dim(all_dense, lax.axis_index("dev"), axis=2, keepdims=False)
    mine = mine.reshape(4, 4, 4, 2, SLOTS, seq_here)
    gate_weight = jnp.stack(
        [
            mine[:, :, :, :, 0].reshape(4, 4, 64),
            mine[:, :, :, :, 1].transpose(2, 0, 1, 3, 4).reshape(4, 4, 64),
            mine[:, :, :, :, 2].transpose(1, 2, 0, 3, 4).reshape(4, 4, 64),
        ]
    )
    gate_weight = jnp.broadcast_to(gate_weight[..., None], gate_weight.shape + (128,))

    queries = select(query_in).reshape(SLOTS, seq_here, HEADS, DH)
    keys_wide = jnp.repeat(
        select(key_in).reshape(SLOTS, seq_here, KV_HEADS, DH), repeat_factor, axis=2
    )
    values_wide = jnp.repeat(
        select(value_in).reshape(SLOTS, seq_here, KV_HEADS, DH), repeat_factor, axis=2
    )
    stacked = jnp.concatenate([queries, keys_wide, values_wide], axis=3)
    attended = attend(lax.all_to_all(stacked, "dev", split_axis=2, concat_axis=1, tiled=True))
    gathered_rows = (
        attended.reshape(SLOTS, dev_count, seq_here, DH)
        .transpose(1, 0, 2, 3)
        .reshape(dev_count * SLOTS * seq_here, DH)
    )
    projected = (
        lax.psum_scatter(
            jnp.dot(gathered_rows, out_proj, preferred_element_type=jnp.float32).astype(
                jnp.bfloat16
            ),
            "dev",
            scatter_dimension=0,
            tiled=True,
        )
        .astype(jnp.float32)
        .reshape(SLOTS, seq_here, features)
    )
    residual = select(states).astype(jnp.float32) + projected
    mean_square = jnp.mean(residual * residual, axis=-1, keepdims=True)
    normed = residual * lax.rsqrt(mean_square + 1e-06) * norm_gain
    halves = normed.reshape(SLOTS, seq_here, 2, 2048).transpose(2, 0, 1, 3)
    hidden, down_sib = expert_hidden(halves, gate_weight, gate_proj[0], up_proj[0], down_proj[0])
    moe = expert_sum(hidden, down_proj[0], down_sib)
    fresh = residual + moe.transpose(1, 2, 0, 3).reshape(SLOTS, seq_here, features)
    reused = states.astype(jnp.float32) + cached_delta.astype(jnp.float32)
    spread = sum(
        jnp.where((place == s)[:, None, None], fresh[s][None], 0.0) for s in range(SLOTS)
    )
    layer_out = jnp.where((recompute == 1)[:, None, None], spread, reused)
    return layer_out.astype(jnp.bfloat16)


def solution(mesh):
    return jax.shard_map(
        on_device,
        mesh=mesh,
        in_specs=(
            P("grp", "dev", None),
            P("grp", "dev", None),
            P("grp", "dev", None),
            P("grp", "dev", None),
            P("grp", "dev", None),
            P("grp"),
            P(("grp", "dev"), None),
            P(("grp", "dev"), None),
            P(),
            P("dev", None),
            P("dev", None, "grp"),
            P("dev", None, "grp"),
            P("dev", "grp", None),
        ),
        out_specs=P("grp", "dev", None),
        check_vma=False,
    )
```

time: 555 us -> 304 us (0.55)
  waiting for transfers between devices: 331 us -> 43.2 us
  Pallas kernels: 0 us -> 161 us
  local copies, waits for them, and re-layouts: 65.9 us -> 10.2 us
  matrix products: 41.8 us -> 5.45 us
  blocking collectives: 81.4 us -> 56.8 us
  starting transfers between devices: 8.05 us -> 0.01 us
  between operations: 13.4 us -> 19.4 us
    pallas_call x0 -> x2, Pallas kernels: none -> 161 us  [the longest x1 86.8 us: expert_hidden(): pl.pallas_call(gather_kernel, out_shape=(jax.ShapeDtypeStruct((2, SLOTS,...]
    reduce_scatter x1 -> x0, waiting for transfers between devices: 98.7 us -> none  [on_device(): lax.psum_scatter(jnp.dot(hidden_val, down_local, preferred_element_type=j...]
    all_gather x1 -> x0, waiting for transfers between devices: 98.2 us -> none  [on_device(): lax.all_gather(arrived, 'grp', axis=0, tiled=True).reshape(-1, features)]
    all_to_all x1 -> x0, blocking collectives: 58 us -> none  [on_device(): lax.all_to_all(outgoing, 'dev', split_axis=0, concat_axis=0, tiled=True)]
    all_to_all x1 -> x0, waiting for transfers between devices: 49.9 us -> none  [on_device(): lax.all_to_all(finished, 'dev', split_axis=0, concat_axis=0, tiled=True)]
    reduce_scatter x1, waiting for transfers between devices: 84.5 us -> 43.1 us  [on_device(): lax.psum_scatter(jnp.dot(gathered_rows, out_proj, preferred_element_type=...]
    all_gather x0 -> x1, blocking collectives: none -> 35.3 us  [on_device(): all_dense = lax.all_gather(dense, ('grp', 'dev'), axis=0, tiled=False)]
    dot_general x3 -> x0, matrix products: 35 us -> none  [the longest x1 13.8 us: on_device(): jnp.dot(hidden_val, down_local, preferred_element_type=jnp.float32)]
  transfers between devices with their start and end apart: 4 -> 1, of which waited for: 4 -> 1; matrix products, arithmetic and copies ran while one was open for 1% -> 1% of each run, Pallas kernels for 0% -> 0%
where the time goes in v1:
time: 304 us
  Pallas kernels  161 us (53%)
  blocking collectives  56.8 us (19%)
  waiting for transfers between devices  43.2 us (14%)
  between operations  19.4 us (6%)
  local copies, waits for them, and re-layouts  10.2 us (3%)
  other arithmetic  7.93 us (3%)
  matrix products  5.45 us (2%)
    pallas_call x1, Pallas kernels, expert_hidden(): pl.pallas_call(gather_kernel, out_shape=(jax.ShapeDtypeStruct((2, SLOTS,...  86.8 us
    pallas_call x1, Pallas kernels, expert_sum(): pl.pallas_call(scatter_kernel, out_shape=jax.ShapeDtypeStruct((2, SLOTS,...  74 us
    reduce_scatter x1, waiting for transfers between devices, on_device(): lax.psum_scatter(jnp.dot(gathered_rows, out_proj, preferred_element_type=...  43.1 us
    all_gather x1, blocking collectives, on_device(): all_dense = lax.all_gather(dense, ('grp', 'dev'), axis=0, tiled=False)  35.3 us
    all_to_all x1, blocking collectives, on_device(): lax.all_to_all(stacked, 'dev', split_axis=2, concat_axis=1, tiled=True)  21.5 us
  transfers between devices with their start and end apart: 1, of which 1 were waited for; matrix products, arithmetic and copies ran while one was open for 1% of the time, Pallas kernels for 0%

profile of v1, /device:TPU:1, one launch (start us, length us, event | category | flops | bytes accessed | tf_op | source)
XLA Modules:
  0.0 303.6 jit_solution(11844570045573012150)
XLA Ops:
  6.5 1.4 fusion.17
  7.9 0.2 reduce-window.19
  8.1 0.8 reduce-window.18
  8.9 1.3 broadcast_compare_fusion.1
  10.3 0.6 fusion.16
  16.6 0.9 constant_dynamic-slice_fusion.14
  17.6 0.8 constant_dynamic-slice_fusion.8
  18.7 0.2 copy.67
  18.9 21.5 %all_to_all.18 = bf16[3,8,32,384]{3,1,0,2:T(8,128)(2,1)S(1)} all-to-all(bf16[3,8,32,384]{3,1,0,2:T(8,128)(2,1)S(1)} %copy.67), channel_id=1, replica_groups=mesh['grp'=4,'dev'=32] {'dev'}, dimensions={2} | all-to-all | bytes 1179648 | tf_op jit(solution)/shard_map/all_to_all | solution.py:561
  40.5 0.4 fusion.18
  40.9 0.6 fusion.3
  41.5 0.2 copy.71
  41.7 4.5 %convolution_convert_fusion = bf16[768,4096]{1,0:T(8,128)(2,1)} fusion(bf16[768,128]{1,0:T(8,128)(2,1)S(1)} %bitcast.116, bf16[128,4096]{1,0:T(8,128)(2,1)S(1)} %copy-done), kind=kOutput, calls=%fused_computation.1 | convolution fusion | flops 808452096 | bytes 7536640 | tf_op jit(solution)/shard_map/dot_general | solution.py:569
  46.2 0.7 copy-done.4
  47.3 0.7 iota_compare_fusion.2
  48.1 0.1 select_reduce_fusion
  48.3 35.3 %all_gather.3 = f32[128,24,32]{2,1,0:T(8,128)S(1)} all-gather(f32[1,24,32]{2,1,0:T(8,128)S(1)} %bitcast_select_fusion), channel_id=1, replica_groups=mesh['grp'=4,'dev'=32] {'grp','dev'}, dimensions={0}, use_global_device_ids=true | all-gather | bytes 396288 | tf_op jit(solution)/shard_map/all_gather | solution.py:541
  83.6 0.9 dynamic-slice_reduce_fusion
  84.5 0.1 reshape.210
  84.7 0.3 slice_reduce_fusion
  85.0 0.1 stack_reshape.6
  85.2 0.1 stack_reshape.7
  85.3 0.1 stack_reshape_squeeze.3
  85.5 43.1 %reduce-scatter.2.cloned.1.call-done = bf16[24,4096]{1,0:T(8,128)(2,1)} async-done(((bf16[768,4096]{1,0:T(8,128)(2,1)}), bf16[24,4096]{1,0:T(8,128)(2,1)}) %reduce-scatter.2.cloned.1.call-update) | async-done | bytes 196624 | tf_op jit(solution)/shard_map/reduce_scatter | solution.py:568
  128.7 1.1 fusion.7
  129.9 1.3 reshape.207
  131.2 1.0 fusion.10.norm_ref
  132.2 1.7 broadcast_in_dim.121.gw_ref
  133.8 86.8 %gather_hidden.1 = (bf16[2,3,4,4,64,768]{5,4,3,2,1,0:T(8,128)(2,1)}, bf16[768,2048]{1,0:T(8,128)(2,1)}) custom-call(f32[2,3,8,2048]{3,2,1,0:T(8,128)} %fusion.10.norm_ref, f32[3,4,4,64,128]{4,3,2,1,0:T(8,128)} %broadcast_in_dim.121.gw_ref, bf16[4096,768]{1,0:T(8,128)(2,1)} %bitcast.112, bf16[4096,768]{1,0:T(8,128)(2,1)} %bitcast.113, bf16[768,4096]{1,0:T(8,128)(2,1)} %bitcast.110), custom_call_target="tpu_custom_call" | custom-call | tf_op jit(solution)/shard_map/gather_hidden/pallas_call | solution.py:279
  220.6 74.0 %down_scatter.1 = f32[2,3,8,2048]{3,2,1,0:T(8,128)} custom-call(bf16[2,3,4,4,64,768]{5,4,3,2,1,0:T(8,128)(2,1)} %get-tuple-element.7.hid_hbm, bf16[768,4096]{1,0:T(8,128)(2,1)} %bitcast.111, bf16[768,2048]{1,0:T(8,128)(2,1)} %get-tuple-element.8.dsib_hbm), custom_call_target="tpu_custom_call" | custom-call | tf_op jit(solution)/shard_map/down_scatter/pallas_call | solution.py:472
  294.6 1.1 copy.81
  295.8 0.9 select_convert_fusion
  (48 shorter events, 1.5 us)
Async XLA Ops:
  6.5 35.2 %copy-start = (bf16[128,4096]{1,0:T(8,128)(2,1)S(1)}, bf16[128,4096]{1,0:T(8,128)(2,1)}, u32[]{:S(2)}) copy-start(bf16[128,4096]{1,0:T(8,128)(2,1)} %param.22) | copy-start | bytes 3145732
  6.5 122.1 %reduce-scatter.2.cloned.1.call-start = ((), (), s32[]{:S(2)}) async-start(), calls=%async_computation.2 | async-start | bytes 6488064 | tf_op jit(solution)/shard_map/reduce_scatter | solution.py:568
  46.1 0.7 copy-start.4
  46.1 0.7 copy-start.5
  46.2 0.9 copy-start.6
  83.6 1.9 copy-start.2
  220.6 75.1 %copy-start.1 = (bf16[24,4096]{1,0:T(8,128)(2,1)S(1)}, bf16[24,4096]{1,0:T(8,128)(2,1)}, u32[]{:S(2)}) copy-start(bf16[24,4096]{1,0:T(8,128)(2,1)} %reduce-scatter.2.cloned.1.call-done) | copy-start | bytes 589828
  294.6 1.2 copy-start.3
Sparse Core Ops, SparseCore 0:
  46.3 82.3 reduce-scatter.1

commit v2 on v1

--- a/solution.py
+++ b/solution.py
@@ -79,9 +79,9 @@
 
 
 def gather_kernel(
-    norm_ref, gw_ref, gate_hbm, up_hbm, down_hbm,
+    norm_ref, route_ref, gate_hbm, up_hbm, down_hbm,
     hid_out, dsib_out,
-    tok, xbuf, wg, wu, hid, send_sem, recv_sem, load_sem, hsend_sem, hrecv_sem, hloc_sem,
+    tok, wg, wu, hid, send_sem, recv_sem, load_sem, hsend_sem, hrecv_sem, hloc_sem,
 ):
     here = Place()
     c = here.core
@@ -100,18 +100,12 @@
     def to(p, axis_at, step):
         return here.to(ORDER[p][axis_at - 1], step)
 
-    swap = copies.start(norm_ref.at[1 - c], xbuf, sib)
     other_half = pl.ds(pl.multiple_of((1 - c) * 2048, 2048), 2048)
     down_copy = copies.start(down_hbm.at[:, other_half], dsib_out, sib)
-    swap.wait_recv()
     pair = pl.ds(2 * c, 2)
     for p in parts:
-        mine, others = norm_ref[c, p], xbuf[p]
-        low = jnp.where(c == 0, mine, others)
-        high = jnp.where(c == 0, others, mine)
-        rows = jnp.concatenate([low, high], axis=0).astype(BF)
-        tok[2 * c, p, m3[p], m2[p], m1[p]] = rows[:, :1024]
-        tok[2 * c + 1, p, m3[p], m2[p], m1[p]] = rows[:, 1024:]
+        for h in range(2):
+            tok[2 * c + h, p, m3[p], m2[p], m1[p]] = norm_ref[h, p]
 
     def send(region, device):
         return copies.start(region, region, device)
@@ -166,7 +160,17 @@
     def hid_piece(p, c3, c2):
         return hid.at[p, c3, c2]
 
+    expert = lax.axis_index("dev")
+    lane = lax.broadcasted_iota(jnp.int32, (64, 128), 1)
+
+    def weight_of(p, c3, c2):
+        index = ((c3, c2), (c2, slice(None), c3), (slice(None), c3, c2))[p]
+        held = route_ref[index].reshape(64, 128)
+        return jnp.sum(jnp.where(lane == p * 32 + expert, held, 0.0), axis=1, keepdims=True)
+
     def ffn(pieces):
+        weights = [weight_of(*piece) for piece in pieces]
+
         def tile(n, carry):
             cols = pl.ds(pl.multiple_of(n * 256, 256), 256)
             gate = jnp.zeros((64 * len(pieces), 256), F32)
@@ -178,8 +182,7 @@
                 up += jnp.dot(rows, wu[depth, cols], preferred_element_type=F32)
             act = gate / (1.0 + jnp.exp(-gate)) * up
             for i, (p, c3, c2) in enumerate(pieces):
-                weight = gw_ref[p, c3, c2][:, :1]
-                hid[p, c3, c2, :, cols] = (act[64 * i : 64 * i + 64] * weight).astype(BF)
+                hid[p, c3, c2, :, cols] = (act[64 * i : 64 * i + 64] * weights[i]).astype(BF)
             return carry
 
         lax.fori_loop(0, 3, tile, 0)
@@ -272,10 +275,10 @@
     pltpu.make_async_copy(hid, hid_out.at[c], hloc_sem).wait()
 
 
-def expert_hidden(norm_halves, gate_weight, gate_w, up_w, down_w):
+def expert_hidden(normed, route, gate_w, up_w, down_w):
     any_space = pl.BlockSpec(memory_space=pl.ANY)
     vmem = pl.BlockSpec(memory_space=pltpu.VMEM)
-    count = 2 + SLOTS * (4 + 4 + 16 + 16)
+    count = 1 + SLOTS * (4 + 4 + 16 + 16)
     return pl.pallas_call(
         gather_kernel,
         out_shape=(
@@ -286,7 +289,6 @@
         out_specs=(any_space, any_space),
         scratch_shapes=[
             pltpu.VMEM((4, SLOTS, 4, 4, 4, 16, 1024), BF),
-            pltpu.VMEM((SLOTS, 8, 2048), F32),
             pltpu.VMEM((4096, 768), BF),
             pltpu.VMEM((4096, 768), BF),
             pltpu.VMEM((SLOTS, 4, 4, 64, 768), BF),
@@ -301,11 +303,11 @@
             collective_id=1, has_side_effects=True, vmem_limit_bytes=60 * 1024 * 1024
         ),
         name="gather_hidden",
-    )(norm_halves, gate_weight, gate_w, up_w, down_w)
+    )(normed, route, gate_w, up_w, down_w)
 
 
 def scatter_kernel(
-    hid_hbm, down_hbm, dsib_hbm,
+    hid_hbm, down_hbm, dsib_hbm, res_ref,
     out_ref,
     hv, dw, part_sum, far3, near3, far2, near2, far1, near1, fin,
     send_sem, recv_sem, load_sem,
@@ -457,6 +459,7 @@
         for q in range(2):
             total = part_sum[q, p, m3[p], m2[p], block(p, 0)].astype(F32)
             total += near1[0, q, p].astype(F32) + near1[1, q, p].astype(F32)
+            total += res_ref[p, :, q * 1024 : q * 1024 + 1024]
             fin[0, p, :, q * 1024 : q * 1024 + 1024] = total[:8]
             fin[1, p, :, q * 1024 : q * 1024 + 1024] = total[8:]
     last = copies.start(fin.at[1 - c], out_ref.at[c], sib)
@@ -465,14 +468,14 @@
     copies.finish()
 
 
-def expert_sum(hidden, down_w, down_sib):
+def expert_sum(hidden, down_w, down_sib, residual):
     any_space = pl.BlockSpec(memory_space=pl.ANY)
     vmem = pl.BlockSpec(memory_space=pltpu.VMEM)
     count = SLOTS * (8 + 16 + 4 + 4) + 1
     return pl.pallas_call(
         scatter_kernel,
         out_shape=jax.ShapeDtypeStruct((2, SLOTS, 8, 2048), F32),
-        in_specs=[any_space, any_space, any_space],
+        in_specs=[any_space, any_space, any_space, vmem],
         out_specs=vmem,
         scratch_shapes=[
             pltpu.VMEM((2, SLOTS, 4, 4, 64, 768), BF),
@@ -493,22 +496,242 @@
             collective_id=2, has_side_effects=True, vmem_limit_bytes=60 * 1024 * 1024
         ),
         name="down_scatter",
-    )(hidden, down_w, down_sib)
-
-
-def attend(packed):
-    query_part = packed[..., :DH]
-    key_part = packed[..., DH : 2 * DH]
-    value_part = packed[..., 2 * DH :]
-    scores = jnp.einsum(
-        "aqhd,akhd->ahqk", query_part, key_part, preferred_element_type=jnp.float32
-    ) * (1.0 / math.sqrt(DH))
-    highest = jnp.max(scores, axis=-1, keepdims=True)
-    raised = jnp.exp(scores - highest)
-    attn_weights = (raised / jnp.sum(raised, axis=-1, keepdims=True)).astype(jnp.bfloat16)
-    return jnp.einsum(
-        "ahqk,akhd->aqhd", attn_weights, value_part, preferred_element_type=jnp.float32
-    ).astype(jnp.bfloat16)
+    )(hidden, down_w, down_sib, residual)
+
+
+def attend(q, k, v):
+    scores = lax.dot_general(q, k, (((1,), (1,)), ((), ())), preferred_element_type=F32)
+    scores = scores * (1.0 / math.sqrt(DH))
+    raised = jnp.exp(scores - jnp.max(scores, axis=-1, keepdims=True))
+    weights = (raised / jnp.sum(raised, axis=-1, keepdims=True)).astype(BF)
+    return jnp.dot(weights, v, preferred_element_type=F32)
+
+
+def attention_kernel(
+    msg, route_ref, state_ref, gain_ref, proj_hbm,
+    norm_out, res_out, route_out,
+    got, mixed, ow, sib_state, part_sum, far_a, near_a, far_b, near_b, squares,
+    send_sem, recv_sem, load_sem,
+):
+    here = Place()
+    c = here.core
+    sib = here.sibling()
+    chip = here.z * 4 + here.x
+
+    my_half = pl.ds(pl.multiple_of(c * 2048, 2048), 2048)
+    other_half = pl.ds(pl.multiple_of((1 - c) * 2048, 2048), 2048)
+    my_rows = pl.ds(pl.multiple_of(c * DH, DH), DH)
+    load = pltpu.make_async_copy(proj_hbm.at[:, my_half], ow.at[my_rows], load_sem)
+    load.start()
+
+    hops = [(dz, dx) for dz in range(4) for dx in range(4) if (dz, dx) != (0, 0)]
+    hops.sort(key=lambda hop: -(min(hop[0], 4 - hop[0]) + min(hop[1], 4 - hop[1])))
+
+    def chip_at(dz, dx):
+        return lax.rem(here.z + dz, 4) * 4 + lax.rem(here.x + dx, 4)
+
+    barrier = pltpu.get_barrier_semaphore()
+    others = [(here.y, chip_at(dz, dx) * 2 + c) for dz, dx in hops]
+    greeted = others + [here.to("y", 1), here.to("y", -1), sib]
+    for other in greeted:
+        pl.semaphore_signal(barrier, inc=1, device_id=other, device_id_type=MESH)
+    pl.semaphore_wait(barrier, len(greeted))
+
+    copies = Copies(send_sem, recv_sem)
+    arriving = []
+    for (dz, dx), other in zip(hops, others):
+        arriving.append(copies.start(msg.at[chip_at(dz, dx)], got.at[c, chip], other))
+    got[c, chip] = msg[chip]
+    route_out[here.y, here.z, here.x, c] = route_ref[...]
+    tile = route_out.at[here.y, here.z, here.x, c]
+    route_swap = copies.start(tile, tile, sib)
+    proj_copy = copies.start(proj_hbm.at[:, other_half], ow.at[my_rows], sib)
+    state_copy = copies.start(state_ref.at[1 - c], sib_state, sib)
+
+    def ring(region, axis):
+        return (copies.start(region, region, here.to(axis, 1)), copies.start(region, region, here.to(axis, -1)))
+
+    route_swap.wait_recv()
+    along_x = ring(route_out.at[here.y, here.z, here.x], "x")
+    for copy in arriving:
+        copy.wait_recv()
+    passed = copies.start(got.at[c], got.at[c], sib)
+    for copy in along_x:
+        copy.wait_recv()
+    left = route_out.at[here.y, here.z, mod4(here.x - 1)]
+    far_x = copies.start(left, left, here.to("x", 1))
+    passed.wait_recv()
+    for s in range(SLOTS):
+        held = got[:, :, s].astype(F32)
+        q = jnp.where(c == 0, held[:, :, 0, :8], held[:, :, 0, 8:]).reshape(256, DH).astype(BF)
+        k = held[:, :, 1, :8].reshape(256, DH).astype(BF)
+        v = held[:, :, 1, 8:].reshape(256, DH).astype(BF)
+        out = attend(q, k, v).reshape(2, 4, 4, 8, DH)
+        mixed[c, :, :, s] = jnp.concatenate([out[0], out[1]], axis=2).astype(BF)
+    mixed_copy = copies.start(mixed.at[c], mixed.at[c], sib)
+    far_x.wait_recv()
+    along_z = ring(route_out.at[here.y, here.z], "z")
+    load.wait()
+    proj_copy.wait_recv()
+    mixed_copy.wait_recv()
+
+    axes = (("z", "x"), ("x", "z"))
+    m2 = [here.at(axes[t][0]) for t in range(2)]
+    m1 = [here.at(axes[t][1]) for t in range(2)]
+
+    def project(t, off):
+        at = mod4(m2[t] + off)
+        rows = [(mixed[h, at] if t == 0 else mixed[h, :, at]).reshape(192, DH) for h in range(2)]
+        rows = jnp.concatenate(rows, axis=1)
+        for half in range(2):
+            first = t * 1024 + half * 512
+            total = jnp.dot(rows, ow[:, first : first + 512], preferred_element_type=F32)
+            part_sum[half, t, at] = total.astype(BF).reshape(4, 48, 512)
+
+    def add(ref, *terms):
+        total = ref[...].astype(F32)
+        for term in terms:
+            total += term[...].astype(F32)
+        ref[...] = total.astype(BF)
+
+    lines = (2, 1, -1, 0)
+    far_copy, near_copy = {}, {}
+    for t in range(2):
+        project(t, 2)
+        at = mod4(m2[t] + 2)
+        for k in range(4):
+            l = mod4(m1[t] + lines[k])
+            far_copy[t, k] = (
+                copies.start(part_sum.at[0, t, at, l], far_a.at[0, t, k], here.to(axes[t][0], 1)),
+                copies.start(part_sum.at[1, t, at, l], far_a.at[1, t, k], here.to(axes[t][0], -1)),
+            )
+    for t in range(2):
+        project(t, 1)
+        project(t, -1)
+    for k in range(4):
+        for t in range(2):
+            l = mod4(m1[t] + lines[k])
+            right, left = mod4(m2[t] + 1), mod4(m2[t] - 1)
+            to_right, to_left = here.to(axes[t][0], 1), here.to(axes[t][0], -1)
+            near_copy[t, k] = [
+                copies.start(part_sum.at[1, t, right, l], near_a.at[0, 1, t, k], to_right),
+                copies.start(part_sum.at[0, t, left, l], near_a.at[1, 0, t, k], to_left),
+            ]
+            for copy in far_copy[t, k]:
+                copy.wait_recv()
+            add(part_sum.at[0, t, right, l], far_a.at[0, t, k])
+            add(part_sum.at[1, t, left, l], far_a.at[1, t, k])
+            near_copy[t, k] += [
+                copies.start(part_sum.at[0, t, right, l], near_a.at[0, 0, t, k], to_right),
+                copies.start(part_sum.at[1, t, left, l], near_a.at[1, 1, t, k], to_left),
+            ]
+        if k == 0:
+            for t in range(2):
+                project(t, 0)
+            for copy in along_z:
+                copy.wait_recv()
+            behind = route_out.at[here.y, mod4(here.z - 1)]
+            far_z = copies.start(behind, behind, here.to("z", 1))
+
+    far_z.wait_recv()
+    along_y = ring(route_out.at[here.y], "y")
+
+    def take_near(t, k):
+        for copy in near_copy[t, k]:
+            copy.wait_recv()
+        l = mod4(m1[t] + lines[k])
+        for half in range(2):
+            add(part_sum.at[half, t, m2[t], l], near_a.at[0, half, t, k], near_a.at[1, half, t, k])
+
+    far_b_copy, near_b_copy = {}, {}
+    for t in range(2):
+        take_near(t, 0)
+        l = mod4(m1[t] + 2)
+        far_b_copy[t] = (
+            copies.start(part_sum.at[0, t, m2[t], l], far_b.at[0, t], here.to(axes[t][1], 1)),
+            copies.start(part_sum.at[1, t, m2[t], l], far_b.at[1, t], here.to(axes[t][1], -1)),
+        )
+    for k, side, step in ((1, 0, 1), (2, 1, -1)):
+        for t in range(2):
+            take_near(t, k)
+            l = mod4(m1[t] + step)
+            far_b_copy[t][side].wait_recv()
+            add(part_sum.at[side, t, m2[t], l], far_b.at[side, t])
+            near_b_copy[t, side] = copies.start(
+                part_sum.at[:, t, m2[t], l], near_b.at[side, :, t], here.to(axes[t][1], step)
+            )
+    for copy in along_y:
+        copy.wait_recv()
+    behind = route_out.at[mod4(here.y - 1)]
+    far_y = copies.start(behind, behind, here.to("y", 1))
+    state_copy.wait_recv()
+    square = jnp.zeros((48, 1), F32)
+    for t in range(2):
+        for copy in near_copy[t, 3]:
+            copy.wait_recv()
+        for side in range(2):
+            near_b_copy[t, side].wait_recv()
+        for half in range(2):
+            total = part_sum[half, t, m2[t], m1[t]].astype(F32)
+            for side in range(2):
+                total += near_a[side, half, t, 3].astype(F32)
+            for side in range(2):
+                total += near_b[side, half, t].astype(F32)
+            first = t * 1024 + half * 512
+            cols = slice(first, first + 512)
+            mine = state_ref[c, :, :, cols]
+            theirs = sib_state[:, :, cols]
+            low = jnp.where(c == 0, mine, theirs)
+            high = jnp.where(c == 0, theirs, mine)
+            total += jnp.concatenate([low, high], axis=1).reshape(48, 512)
+            res_out[:, :, cols] = total.reshape(SLOTS, 16, 512)
+            square += jnp.sum(total * total, axis=1, keepdims=True)
+    squares[c] = jnp.broadcast_to(square, (48, 128))
+    square_copy = copies.start(squares.at[c], squares.at[c], sib)
+    square_copy.wait_recv()
+    mean = (squares[0, :, :1] + squares[1, :, :1]) * (1.0 / 4096.0)
+    factor = lax.rsqrt(mean + 1e-06).reshape(SLOTS, 16, 1)
+    for h in range(2):
+        cols = slice(h * 1024, h * 1024 + 1024)
+        gain = gain_ref[pl.ds(c, 1), cols].reshape(1, 1, 1024)
+        norm_out[h] = (res_out[:, :, cols] * factor * gain).astype(BF)
+    far_y.wait_recv()
+    copies.finish()
+
+
+def attention(msg, route, state, gain, out_proj):
+    any_space = pl.BlockSpec(memory_space=pl.ANY)
+    vmem = pl.BlockSpec(memory_space=pltpu.VMEM)
+    count = 15 + 1 + 1 + 1 + 1 + 1 + 2 * (8 + 16 + 2 + 2) + 9 + 1
+    return pl.pallas_call(
+        attention_kernel,
+        out_shape=(
+            jax.ShapeDtypeStruct((2, SLOTS, 16, 1024), BF),
+            jax.ShapeDtypeStruct((SLOTS, 16, 2048), F32),
+            jax.ShapeDtypeStruct((4, 4, 4, 2, 8, 128), F32),
+        ),
+        in_specs=[vmem, vmem, vmem, vmem, any_space],
+        out_specs=(vmem, vmem, vmem),
+        scratch_shapes=[
+            pltpu.VMEM((2, 16, SLOTS, 2, 16, DH), BF),
+            pltpu.VMEM((2, 4, 4, SLOTS, 16, DH), BF),
+            pltpu.VMEM((2 * DH, 2048), BF),
+            pltpu.VMEM((SLOTS, 8, 2048), F32),
+            pltpu.VMEM((2, 2, 4, 4, 48, 512), BF),
+            pltpu.VMEM((2, 2, 4, 48, 512), BF),
+            pltpu.VMEM((2, 2, 2, 4, 48, 512), BF),
+            pltpu.VMEM((2, 2, 48, 512), BF),
+            pltpu.VMEM((2, 2, 2, 48, 512), BF),
+            pltpu.VMEM((2, 48, 128), F32),
+            pltpu.SemaphoreType.DMA((count,)),
+            pltpu.SemaphoreType.DMA((count,)),
+            pltpu.SemaphoreType.DMA,
+        ],
+        compiler_params=pltpu.CompilerParams(
+            collective_id=3, has_side_effects=True, vmem_limit_bytes=48 * 1024 * 1024
+        ),
+        name="attention_norm",
+    )(msg, route, state, gain, out_proj)
 
 
 def on_device(
@@ -517,7 +740,6 @@
 ):
     dev_count = lax.axis_size("dev")
     req_here, seq_here, features = states.shape
-    repeat_factor = HEADS // KV_HEADS
     rank = jnp.cumsum(recompute) - 1
     live_count = jnp.sum(recompute)
     idle_rank = live_count + jnp.cumsum(1 - recompute) - 1
@@ -537,52 +759,24 @@
     dense = jnp.sum(
         jnp.where(ids[..., None] == experts, weights[..., None], 0.0), axis=2
     )
-    dense = jnp.where(live_slot[:, None, None], dense, 0.0).reshape(SLOTS * seq_here, dev_count)
-    all_dense = lax.all_gather(dense, ("grp", "dev"), axis=0, tiled=False)
-    mine = lax.dynamic_index_in_dim(all_dense, lax.axis_index("dev"), axis=2, keepdims=False)
-    mine = mine.reshape(4, 4, 4, 2, SLOTS, seq_here)
-    gate_weight = jnp.stack(
-        [
-            mine[:, :, :, :, 0].reshape(4, 4, 64),
-            mine[:, :, :, :, 1].transpose(2, 0, 1, 3, 4).reshape(4, 4, 64),
-            mine[:, :, :, :, 2].transpose(1, 2, 0, 3, 4).reshape(4, 4, 64),
-        ]
+    dense = jnp.where(live_slot[:, None, None], dense, 0.0)
+    route = dense.transpose(1, 0, 2).reshape(seq_here, -1)
+    route = jnp.pad(route, ((0, 0), (0, 128 - SLOTS * dev_count)))
+
+    chips = dev_count // 2
+    queries = select(query_in).reshape(SLOTS, seq_here, chips, 2, DH).transpose(2, 0, 3, 1, 4)
+    keys = select(key_in).reshape(SLOTS, seq_here, KV_HEADS, DH)
+    values = select(value_in).reshape(SLOTS, seq_here, KV_HEADS, DH)
+    both = jnp.stack([keys, values]).transpose(3, 1, 0, 2, 4)
+    both = jnp.repeat(both, chips // KV_HEADS, axis=0)
+    msg = jnp.stack(
+        [queries.reshape(chips, SLOTS, 16, DH), both.reshape(chips, SLOTS, 16, DH)], axis=2
     )
-    gate_weight = jnp.broadcast_to(gate_weight[..., None], gate_weight.shape + (128,))
-
-    queries = select(query_in).reshape(SLOTS, seq_here, HEADS, DH)
-    keys_wide = jnp.repeat(
-        select(key_in).reshape(SLOTS, seq_here, KV_HEADS, DH), repeat_factor, axis=2
-    )
-    values_wide = jnp.repeat(
-        select(value_in).reshape(SLOTS, seq_here, KV_HEADS, DH), repeat_factor, axis=2
-    )
-    stacked = jnp.concatenate([queries, keys_wide, values_wide], axis=3)
-    attended = attend(lax.all_to_all(stacked, "dev", split_axis=2, concat_axis=1, tiled=True))
-    gathered_rows = (
-        attended.reshape(SLOTS, dev_count, seq_here, DH)
-        .transpose(1, 0, 2, 3)
-        .reshape(dev_count * SLOTS * seq_here, DH)
-    )
-    projected = (
-        lax.psum_scatter(
-            jnp.dot(gathered_rows, out_proj, preferred_element_type=jnp.float32).astype(
-                jnp.bfloat16
-            ),
-            "dev",
-            scatter_dimension=0,
-            tiled=True,
-        )
-        .astype(jnp.float32)
-        .reshape(SLOTS, seq_here, features)
-    )
-    residual = select(states).astype(jnp.float32) + projected
-    mean_square = jnp.mean(residual * residual, axis=-1, keepdims=True)
-    normed = residual * lax.rsqrt(mean_square + 1e-06) * norm_gain
-    halves = normed.reshape(SLOTS, seq_here, 2, 2048).transpose(2, 0, 1, 3)
-    hidden, down_sib = expert_hidden(halves, gate_weight, gate_proj[0], up_proj[0], down_proj[0])
-    moe = expert_sum(hidden, down_proj[0], down_sib)
-    fresh = residual + moe.transpose(1, 2, 0, 3).reshape(SLOTS, seq_here, features)
+    state = select(states).astype(F32).reshape(SLOTS, seq_here, 2, 2048).transpose(2, 0, 1, 3)
+    normed, residual, routes = attention(msg, route, state, norm_gain.reshape(2, 2048), out_proj)
+    hidden, down_sib = expert_hidden(normed, routes, gate_proj[0], up_proj[0], down_proj[0])
+    fresh = expert_sum(hidden, down_proj[0], down_sib, residual)
+    fresh = fresh.transpose(1, 2, 0, 3).reshape(SLOTS, seq_here, features)
     reused = states.astype(jnp.float32) + cached_delta.astype(jnp.float32)
     spread = sum(
         jnp.where((place == s)[:, None, None], fresh[s][None], 0.0) for s in range(SLOTS)

time: 304 us -> 224 us (0.74)
  blocking collectives: 56.8 us -> 0 us
  waiting for transfers between devices: 43.2 us -> 0 us
  Pallas kernels: 161 us -> 202 us
  between operations: 19.4 us -> 5.78 us
  matrix products: 5.45 us -> 0 us
    reduce_scatter x1 -> x0, waiting for transfers between devices: 43.1 us -> none  [on_device(): lax.psum_scatter(jnp.dot(gathered_rows, out_proj, preferred_element_type=...]
    pallas_call x0 -> x1, Pallas kernels: none -> 42 us  [attention(): pl.pallas_call(attention_kernel, out_shape=(jax.ShapeDtypeStruct((2, SLOT...]
    all_gather x1 -> x0, blocking collectives: 35.3 us -> none  [on_device(): all_dense = lax.all_gather(dense, ('grp', 'dev'), axis=0, tiled=False)]
    all_to_all x1 -> x0, blocking collectives: 21.5 us -> none  [on_device(): lax.all_to_all(stacked, 'dev', split_axis=2, concat_axis=1, tiled=True)]
    dot_general x2 -> x0, matrix products: 5.05 us -> none  [the longest x1 4.45 us: on_device(): jnp.dot(gathered_rows, out_proj, preferred_element_type=jnp.float32)]
  transfers between devices with their start and end apart: 1 -> 0, of which waited for: 1 -> 0; matrix products, arithmetic and copies ran while one was open for 1% -> 0% of each run, Pallas kernels for 0% -> 0%
where the time goes in v2:
time: 224 us; the launch traced here: 223 us
  Pallas kernels  202 us (90%)
  local copies, waits for them, and re-layouts  9.64 us (4%)
  between operations  5.78 us (3%)
  other arithmetic  5.66 us (3%)
    pallas_call x1, Pallas kernels, expert_hidden(): pl.pallas_call(gather_kernel, out_shape=(jax.ShapeDtypeStruct((2, SLOTS,...  84.9 us
    pallas_call x1, Pallas kernels, expert_sum(): pl.pallas_call(scatter_kernel, out_shape=jax.ShapeDtypeStruct((2, SLOTS,...  75.3 us
    pallas_call x1, Pallas kernels, attention(): pl.pallas_call(attention_kernel, out_shape=(jax.ShapeDtypeStruct((2, SLOT...  42 us

profile of v2, /device:TPU:1, one launch (start us, length us, event | category | flops | bytes accessed | tf_op | source)
XLA Modules:
  0.0 223.3 jit_solution(18350805070782494250)
XLA Ops:
  0.0 1.3 fusion.2
  1.3 0.2 reduce-window.19
  1.5 0.8 reduce-window.18
  2.3 1.3 broadcast_compare_fusion.1
  3.6 0.1 select_reduce_fusion.1
  3.7 0.6 fusion.1
  9.9 1.0 constant_dynamic-slice_fusion.2
  11.0 0.8 constant_dynamic-slice_fusion.11
  12.0 0.8 reshape.94
  12.8 0.1 copy.24
  12.9 0.8 reshape.95
  13.7 0.1 copy.25
  13.8 0.1 select_reduce_fusion
  13.9 0.7 iota_compare_fusion.2
  14.6 0.1 select_bitcast_fusion
  14.7 0.1 reshape.96
  14.8 0.7 reshape.97.gain_ref
  15.5 0.0 copy-start
  15.5 1.2 copy-done
  16.7 42.0 %attention_norm.1 = (bf16[2,3,16,1024]{3,2,1,0:T(8,128)(2,1)S(1)}, f32[3,16,2048]{2,1,0:T(8,128)S(1)}, f32[4,4,4,2,8,128]{5,4,3,2,1,0:T(8,128)S(1)}) custom-call(bf16[16,3,2,16,128]{4,3,2,1,0:T(8,128)(2,1)S(1)} %pad_maximum_fusion.msg, f32[8,128]{1,0:T(8,128)S(1)} %pad.4.route_ref, f32[2,3,8,2048]{3,2,1,0:T(8,128)S(1)} %convert_bitcast_fusion.state_ref, ...), custom_call_target="tpu_custom_call" | custom-call | tf_op jit(solution)/shard_map/attention_norm/pallas_call | solution.py:706
  58.8 0.0 copy-start.1
  58.8 0.8 copy-done.1
  59.6 0.8 copy-done.2
  60.4 0.7 copy-done.3
  61.1 84.9 %gather_hidden.1 = (bf16[2,3,4,4,64,768]{5,4,3,2,1,0:T(8,128)(2,1)}, bf16[768,2048]{1,0:T(8,128)(2,1)}) custom-call(bf16[2,3,16,1024]{3,2,1,0:T(8,128)(2,1)} %copy-done.3, f32[4,4,4,2,8,128]{5,4,3,2,1,0:T(8,128)} %copy-done.1, bf16[4096,768]{1,0:T(8,128)(2,1)} %bitcast.45, bf16[4096,768]{1,0:T(8,128)(2,1)} %bitcast.46, bf16[768,4096]{1,0:T(8,128)(2,1)} %bitcast.43), custom_call_target="tpu_custom_call" | custom-call | tf_op jit(solution)/shard_map/gather_hidden/pallas_call | solution.py:282
  146.0 0.0 copy-start.4
  146.0 0.0 copy-start.5
  146.0 75.3 %down_scatter.1 = f32[2,3,8,2048]{3,2,1,0:T(8,128)} custom-call(bf16[2,3,4,4,64,768]{5,4,3,2,1,0:T(8,128)(2,1)} %get-tuple-element.12.hid_hbm, bf16[768,4096]{1,0:T(8,128)(2,1)} %bitcast.44, bf16[768,2048]{1,0:T(8,128)(2,1)} %get-tuple-element.13.dsib_hbm, f32[3,16,2048]{2,1,0:T(8,128)} %copy-done.2), custom_call_target="tpu_custom_call" | custom-call | tf_op jit(solution)/shard_map/down_scatter/pallas_call | solution.py:475
  221.3 1.1 fusion
  222.4 0.0 copy-done.4
  222.4 0.0 copy-done.5
  222.4 0.9 select_convert_fusion
  (18 shorter events, 0.3 us)
Async XLA Ops:
  15.5 1.2 copy-start
  58.8 0.8 copy-start.1
  59.6 0.8 copy-start.2
  60.4 0.7 copy-start.3
  146.0 76.4 %copy-start.4 = (bf16[4,8,4096]{2,1,0:T(8,128)(2,1)S(1)}, bf16[4,8,4096]{2,1,0:T(8,128)(2,1)}, u32[]{:S(2)}) copy-start(bf16[4,8,4096]{2,1,0:T(8,128)(2,1)} %param.13) | copy-start | bytes 786436
  146.0 76.4 %copy-start.5 = (bf16[4,8,4096]{2,1,0:T(8,128)(2,1)S(1)}, bf16[4,8,4096]{2,1,0:T(8,128)(2,1)}, u32[]{:S(2)}) copy-start(bf16[4,8,4096]{2,1,0:T(8,128)(2,1)} %param.17) | copy-start | bytes 786436

commit v3 on v2

--- a/solution.py
+++ b/solution.py
@@ -101,7 +101,6 @@
         return here.to(ORDER[p][axis_at - 1], step)
 
     other_half = pl.ds(pl.multiple_of((1 - c) * 2048, 2048), 2048)
-    down_copy = copies.start(down_hbm.at[:, other_half], dsib_out, sib)
     pair = pl.ds(2 * c, 2)
     for p in parts:
         for h in range(2):
@@ -246,18 +245,19 @@
         own_line[p][3] = send(region, sib)
     forward(0)
     own_unit((2, 3))
+    down_copy = copies.start(down_hbm.at[:, other_half], dsib_out, sib)
     forward(1)
     near_unit(0)
     forward(2)
-    settle(0)
     near_unit(1)
     forward(3)
+    near_unit(2)
+    settle(0)
     settle(1)
-    near_unit(2)
+    near_unit(3)
+    settle(2)
+    settle(3)
     far_unit((0, 1))
-    settle(2)
-    near_unit(3)
-    settle(3)
     far_unit((2, 3))
 
     copies.finish()
@@ -349,14 +349,13 @@
         loaded_h[off, p].wait()
 
         def tile(n, carry):
-            cols = pl.ds(pl.multiple_of(n * 512, 512), 512)
+            cols = pl.ds(pl.multiple_of(n * 1024, 1024), 1024)
             total = jnp.dot(hv[0, p, at].reshape(256, 768), dw[0, :, cols], preferred_element_type=F32)
             total += jnp.dot(hv[1, p, at].reshape(256, 768), dw[1, :, cols], preferred_element_type=F32)
-            into = pl.ds(pl.multiple_of(lax.rem(n, 2) * 512, 512), 512)
-            part_sum[lax.div(n, 2), p, at, :, :, into] = total.astype(BF).reshape(4, 64, 512)
+            part_sum[n, p, at] = total.astype(BF).reshape(4, 64, 1024)
             return carry
 
-        lax.fori_loop(0, 4, tile, 0)
+        lax.fori_loop(0, 2, tile, 0)
 
     def add(ref, *others):
         total = ref[...].astype(F32)
@@ -369,44 +368,34 @@
     def at_line(p, k):
         return mod4(m2[p] + lines[k])
 
-    far_copy = {}
-    for p in parts:
-        down(p, 2)
-        at = mod4(m3[p] + 2)
-        for k in range(4):
-            l = at_line(p, k)
-            far_copy[p, k] = (
-                copies.start(part_sum.at[0, p, at, l], far3.at[0, p, k], to(p, 3, 1)),
-                copies.start(part_sum.at[1, p, at, l], far3.at[1, p, k], to(p, 3, -1)),
-            )
-    for p in parts:
-        down(p, 1)
-        down(p, -1)
-    near_copy = {}
-
-    def pass_near(k):
-        for p in parts:
-            l = at_line(p, k)
-            right, left = mod4(m3[p] + 1), mod4(m3[p] - 1)
-            near_copy[p, k] = [
-                copies.start(part_sum.at[1, p, right, l], near3.at[0, 1, p, k], to(p, 3, 1)),
-                copies.start(part_sum.at[0, p, left, l], near3.at[1, 0, p, k], to(p, 3, -1)),
-            ]
-            for copy in far_copy[p, k]:
-                copy.wait_recv()
-            add(part_sum.at[0, p, right, l], far3.at[0, p, k])
-            add(part_sum.at[1, p, left, l], far3.at[1, p, k])
-            near_copy[p, k] += [
-                copies.start(part_sum.at[0, p, right, l], near3.at[0, 0, p, k], to(p, 3, 1)),
-                copies.start(part_sum.at[1, p, left, l], near3.at[1, 1, p, k], to(p, 3, -1)),
-            ]
-
-    pass_near(0)
-    for p in parts:
-        down(p, 0)
-    pass_near(1)
-    pass_near(2)
-    pass_near(3)
+    far_copy, near_copy = {}, {}
+
+    def pass_far(p, k):
+        at, l = mod4(m3[p] + 2), at_line(p, k)
+        far_copy[p, k] = (
+            copies.start(part_sum.at[0, p, at, l], far3.at[0, p, k], to(p, 3, 1)),
+            copies.start(part_sum.at[1, p, at, l], far3.at[1, p, k], to(p, 3, -1)),
+        )
+
+    def pass_free(p, k):
+        l = at_line(p, k)
+        right, left = mod4(m3[p] + 1), mod4(m3[p] - 1)
+        near_copy[p, k] = [
+            copies.start(part_sum.at[1, p, right, l], near3.at[0, 1, p, k], to(p, 3, 1)),
+            copies.start(part_sum.at[0, p, left, l], near3.at[1, 0, p, k], to(p, 3, -1)),
+        ]
+
+    def pass_bound(p, k):
+        l = at_line(p, k)
+        right, left = mod4(m3[p] + 1), mod4(m3[p] - 1)
+        for copy in far_copy[p, k]:
+            copy.wait_recv()
+        add(part_sum.at[0, p, right, l], far3.at[0, p, k])
+        add(part_sum.at[1, p, left, l], far3.at[1, p, k])
+        near_copy[p, k] += [
+            copies.start(part_sum.at[0, p, right, l], near3.at[0, 0, p, k], to(p, 3, 1)),
+            copies.start(part_sum.at[1, p, left, l], near3.at[1, 1, p, k], to(p, 3, -1)),
+        ]
 
     def take_near(p, k):
         for copy in near_copy[p, k]:
@@ -414,6 +403,20 @@
         for q in range(2):
             add(part_sum.at[q, p, m3[p], at_line(p, k)], near3.at[0, q, p, k], near3.at[1, q, p, k])
 
+    for p in parts:
+        down(p, 2)
+        for k in range(4):
+            pass_far(p, k)
+    for p in parts:
+        down(p, 1)
+        down(p, -1)
+        for k in range(4):
+            pass_free(p, k)
+    for k in range(2):
+        for p in parts:
+            pass_bound(p, k)
+    for p in parts:
+        down(p, 0)
     far2_copy, near2_copy = {}, {}
     for p in parts:
         take_near(p, 0)
@@ -422,6 +425,9 @@
             copies.start(part_sum.at[0, p, m3[p], l], far2.at[0, p], to(p, 2, 1)),
             copies.start(part_sum.at[1, p, m3[p], l], far2.at[1, p], to(p, 2, -1)),
         )
+    for k in (2, 3):
+        for p in parts:
+            pass_bound(p, k)
     for k, side in ((1, 0), (2, 1)):
         for p in parts:
             take_near(p, k)
@@ -438,6 +444,7 @@
 
     for p in parts:
         take_near(p, 3)
+    for p in parts:
         for side in range(2):
             near2_copy[p, side].wait_recv()
         for q in range(2):

time: 224 us -> 208 us (0.929)
  Pallas kernels: 202 us -> 186 us
    pallas_call x1, Pallas kernels: 75.3 us -> 66.8 us  [expert_sum(): pl.pallas_call(scatter_kernel, out_shape=jax.ShapeDtypeStruct((2, SLOTS,...]
    pallas_call x1, Pallas kernels: 84.9 us -> 77.2 us  [expert_hidden(): pl.pallas_call(gather_kernel, out_shape=(jax.ShapeDtypeStruct((2, SLOTS,...]
where the time goes in v3:
time: 208 us; the launch traced here: 207 us
  Pallas kernels  186 us (89%)
  local copies, waits for them, and re-layouts  9.64 us (5%)
  between operations  5.78 us (3%)
  other arithmetic  5.66 us (3%)
    pallas_call x1, Pallas kernels, expert_hidden(): pl.pallas_call(gather_kernel, out_shape=(jax.ShapeDtypeStruct((2, SLOTS,...  77.2 us
    pallas_call x1, Pallas kernels, expert_sum(): pl.pallas_call(scatter_kernel, out_shape=jax.ShapeDtypeStruct((2, SLOTS,...  66.8 us
    pallas_call x1, Pallas kernels, attention(): pl.pallas_call(attention_kernel, out_shape=(jax.ShapeDtypeStruct((2, SLOT...  42 us

profile of v3, /device:TPU:1, one launch (start us, length us, event | category | flops | bytes accessed | tf_op | source)
XLA Modules:
  0.0 207.1 jit_solution(13101027467383847177)
XLA Ops:
  0.0 1.3 fusion.2
  1.3 0.2 reduce-window.19
  1.5 0.8 reduce-window.18
  2.3 1.3 broadcast_compare_fusion.1
  3.6 0.1 select_reduce_fusion.1
  3.7 0.6 fusion.1
  9.9 1.0 constant_dynamic-slice_fusion.2
  11.0 0.8 constant_dynamic-slice_fusion.11
  12.0 0.8 reshape.94
  12.8 0.1 copy.24
  12.9 0.8 reshape.95
  13.7 0.1 copy.25
  13.8 0.1 select_reduce_fusion
  13.9 0.7 iota_compare_fusion.2
  14.6 0.1 select_bitcast_fusion
  14.7 0.1 reshape.96
  14.8 0.7 reshape.97.gain_ref
  15.5 0.0 copy-start
  15.5 1.2 copy-done
  16.7 42.0 %attention_norm.1 = (bf16[2,3,16,1024]{3,2,1,0:T(8,128)(2,1)S(1)}, f32[3,16,2048]{2,1,0:T(8,128)S(1)}, f32[4,4,4,2,8,128]{5,4,3,2,1,0:T(8,128)S(1)}) custom-call(bf16[16,3,2,16,128]{4,3,2,1,0:T(8,128)(2,1)S(1)} %pad_maximum_fusion.msg, f32[8,128]{1,0:T(8,128)S(1)} %pad.4.route_ref, f32[2,3,8,2048]{3,2,1,0:T(8,128)S(1)} %convert_bitcast_fusion.state_ref, ...), custom_call_target="tpu_custom_call" | custom-call | tf_op jit(solution)/shard_map/attention_norm/pallas_call | solution.py:713
  58.8 0.0 copy-start.1
  58.8 0.8 copy-done.1
  59.6 0.8 copy-done.2
  60.4 0.7 copy-done.3
  61.1 77.2 %gather_hidden.1 = (bf16[2,3,4,4,64,768]{5,4,3,2,1,0:T(8,128)(2,1)}, bf16[768,2048]{1,0:T(8,128)(2,1)}) custom-call(bf16[2,3,16,1024]{3,2,1,0:T(8,128)(2,1)} %copy-done.3, f32[4,4,4,2,8,128]{5,4,3,2,1,0:T(8,128)} %copy-done.1, bf16[4096,768]{1,0:T(8,128)(2,1)} %bitcast.45, bf16[4096,768]{1,0:T(8,128)(2,1)} %bitcast.46, bf16[768,4096]{1,0:T(8,128)(2,1)} %bitcast.43), custom_call_target="tpu_custom_call" | custom-call | tf_op jit(solution)/shard_map/gather_hidden/pallas_call | solution.py:282
  138.2 0.0 copy-start.4
  138.2 0.0 copy-start.5
  138.3 66.8 %down_scatter.1 = f32[2,3,8,2048]{3,2,1,0:T(8,128)} custom-call(bf16[2,3,4,4,64,768]{5,4,3,2,1,0:T(8,128)(2,1)} %get-tuple-element.12.hid_hbm, bf16[768,4096]{1,0:T(8,128)(2,1)} %bitcast.44, bf16[768,2048]{1,0:T(8,128)(2,1)} %get-tuple-element.13.dsib_hbm, f32[3,16,2048]{2,1,0:T(8,128)} %copy-done.2), custom_call_target="tpu_custom_call" | custom-call | tf_op jit(solution)/shard_map/down_scatter/pallas_call | solution.py:482
  205.1 1.1 fusion
  206.1 0.0 copy-done.4
  206.1 0.0 copy-done.5
  206.2 0.9 select_convert_fusion
  (18 shorter events, 0.3 us)
Async XLA Ops:
  15.5 1.2 copy-start
  58.8 0.8 copy-start.1
  59.6 0.8 copy-start.2
  60.4 0.7 copy-start.3
  138.2 67.9 %copy-start.4 = (bf16[4,8,4096]{2,1,0:T(8,128)(2,1)S(1)}, bf16[4,8,4096]{2,1,0:T(8,128)(2,1)}, u32[]{:S(2)}) copy-start(bf16[4,8,4096]{2,1,0:T(8,128)(2,1)} %param.13) | copy-start | bytes 786436
  138.2 67.9 %copy-start.5 = (bf16[4,8,4096]{2,1,0:T(8,128)(2,1)S(1)}, bf16[4,8,4096]{2,1,0:T(8,128)(2,1)}, u32[]{:S(2)}) copy-start(bf16[4,8,4096]{2,1,0:T(8,128)(2,1)} %param.17) | copy-start | bytes 786436
